TPU v7x, 256 devices: a whole 4x4x8 slice. The times are simulated.
256 devices in a mesh: space: 64 (over x, y_hi, z), kern: 4 (over y_lo, core).
Axes of the slice: x: 4, y: 4 (y_hi: 2, y_lo: 2; y = y_hi * 2 + y_lo), z: 8, core: 2. Of those that a mesh axis runs over, the one named last changes fastest.
Arguments:
- phase: float32 [512, 8192], P(None, 'space'), may hold values from -3.140625 to 3.140625
- target: int32 [512, 8192], P(None, 'space'), may hold values 0 or 1
- kernels: float32 [2, 16, 129, 129], P(None, 'kern'), may hold values from -0.046875 to 0.046875
- weights: float32 [16], P('kern'), may hold values from 0.01 to 0.25
Outputs:
- resist: float32 [512, 8192], P('kern', 'space')
- grad_phase: float32 [512, 8192], P('kern', 'space')
All inputs are finite; a program needn't handle non-finite values. No bound on the sum of `target` on one device may be relied on, other than what follows from the above.
Results may differ from a plain program's by a relative error of at most 0.0003.
Values sent between devices are 32-bit elements; how exact they have to be, the bound alone decides.
A program may use at most 64 MiB of HBM per device.

v0:
```python
import functools

import jax
import jax.numpy as jnp
import ml_dtypes
import numpy as np
from jax import lax
from jax.experimental import pallas as pl
from jax.experimental.pallas import tpu as pltpu
from jax.sharding import PartitionSpec as P

STEEP = 2.5
LEVEL = 2.0
N = 128
H = 64
F32 = jnp.float32
BF16 = jnp.bfloat16
MESH = pl.DeviceIdType.MESH


def tables():
    x = np.arange(N)[:, None]
    k = np.arange(N)[None, :]
    parts = []
    for parity in (0, 1):
        angle = -2.0 * np.pi / (2 * N) * ((2 * k + parity) * x % (2 * N))
        c, s = np.cos(angle), np.sin(angle)
        parts.append(np.block([[c, s], [-s, c]]))
    full = np.concatenate(parts, axis=1)
    high = full.astype(ml_dtypes.bfloat16)
    low = (full - high.astype(np.float64)).astype(ml_dtypes.bfloat16)
    return high, low, np.ascontiguousarray(high.T), np.ascontiguousarray(low.T)


def cat(parts, axis):
    return jnp.concatenate(parts, axis=axis)


def split(x):
    high = x.astype(BF16)
    return high, (x - high.astype(F32)).astype(BF16)


def dot(a, b):
    return jnp.dot(a, b, preferred_element_type=F32)


def right(x, high, low):
    xh, xl = split(x)
    return dot(cat([xh, xl, xh], 1), cat([high, high, low], 0))


def left(high, low, x):
    xh, xl = split(x)
    return dot(cat([high, high, low], 1), cat([xh, xl, xh], 0))


def sincos(x):
    turn = jnp.floor(x * (2.0 / np.pi) + 0.5)
    r = x - turn * 1.5707855224609375
    r = r - turn * 1.0804273188e-05
    q = turn.astype(jnp.int32)
    z = r * r
    s = r + r * z * (-1.6666654611e-1 + z * (8.3321608736e-3 + z * -1.9515295891e-4))
    c = 1.0 - 0.5 * z + z * z * (
        4.166664568298827e-2 + z * (-1.388731625493765e-3 + z * 2.443315711809948e-5)
    )
    swap = (q & 1) != 0
    sin = jnp.where(swap, c, s)
    cos = jnp.where(swap, s, c)
    sin = jnp.where((q & 2) != 0, -sin, sin)
    cos = jnp.where(((q + 1) & 2) != 0, -cos, cos)
    return sin, cos


def flip(index, step):
    return index + step - 2 * step * lax.rem(index // step, 2)


def kernel(
    space, groups, far,
    phase_ref, target_ref, kern_ref, weight_ref, fch, fcl, frh, frl,
    resist_ref, grad_ref,
    window, halo_out, halo_in, trig, raw, resp, spec, field, acc, yield_, gout, pout, rin,
    halo_s, halo_r, kern_s, kern_r, rim_s, rim_r,
):
    rows = phase_ref.shape[0]
    count = kern_ref.shape[1]
    tall = N + 8
    my_s = lax.axis_index("space")
    my_k = lax.axis_index("kern")
    s_next = lax.rem(my_s + 1, space)
    s_prev = lax.rem(my_s + space - 1, space)
    k_next = lax.rem(my_k + 1, groups)
    k_prev = lax.rem(my_k + groups - 1, groups)
    sibling = (my_s, flip(my_k, 1))
    across = (my_s, flip(my_k, 2))
    around = (flip(my_s, far), flip(my_k, 2))

    barrier = pltpu.get_barrier_semaphore()
    greeted = [
        (s_next, my_k), (s_prev, my_k), sibling, across, (my_s, flip(flip(my_k, 1), 2)), around,
        (s_next, k_next), (s_next, k_prev), (s_prev, k_next), (s_prev, k_prev),
    ]
    for device in greeted:
        pl.semaphore_signal(barrier, inc=1, device_id=device, device_id_type=MESH)

    lane = lax.broadcasted_iota(jnp.int32, (8, N), 1)[:1]

    def pack(upper, lower):
        turned = pltpu.roll(lower, H, 1)
        return jnp.where(lane < H, upper, turned), jnp.where(lane < H, turned, upper)

    def unpack(low_side, high_side):
        upper = jnp.where(lane < H, low_side, high_side)
        return upper, pltpu.roll(jnp.where(lane < H, high_side, low_side), H, 1)

    def remote(src, dst, ssem, rsem, device):
        return pltpu.make_async_remote_copy(
            src_ref=src, dst_ref=dst, send_sem=ssem, recv_sem=rsem,
            device_id=device, device_id_type=MESH,
        )

    own = pl.multiple_of(my_k * N, N)
    after = pl.multiple_of(jnp.minimum(own + N, rows - H), H)
    before = pl.multiple_of(jnp.maximum(own - H, 0), H)
    window[0:N] = phase_ref[pl.ds(own, N)]
    window[N : N + H] = phase_ref[pl.ds(after, H)]
    window[N + H :] = phase_ref[pl.ds(before, H)]
    halo_out[0], halo_out[1] = pack(window[:N], window[N:])
    halo = [
        remote(halo_out.at[0], halo_in.at[0], halo_s.at[0], halo_r.at[0], (s_prev, my_k)),
        remote(halo_out.at[1], halo_in.at[1], halo_s.at[1], halo_r.at[1], (s_next, my_k)),
    ]

    gains = [
        jnp.sqrt(jnp.zeros((1, N), F32) + weight_ref[n]) * 2.0**-16 for n in range(count)
    ]
    for part in range(2):
        edges = jnp.zeros((8, N), F32)
        for n in range(count):
            gain = gains[n]
            raw[my_k, part, tall * n : tall * n + N] = (
                pltpu.roll(kern_ref[part, n, 0:N, 0:N], H, 1) * gain
            )
            last = jnp.broadcast_to(kern_ref[part, n, N : N + 1, 0:N], (8, N))
            raw[my_k, part, tall * n + N : tall * (n + 1)] = pltpu.roll(last, H, 1) * gain
            for g in range(N // 8 + 1):
                end = 8 * g + 8 if g < N // 8 else N + 1
                column = kern_ref[part, n, 8 * g : end, N : N + 1]
                edges = jnp.where(lane == count * g + n, column * gain, edges)
        raw[my_k, part, tall * count :] = edges

    pl.semaphore_wait(barrier, len(greeted))
    for copy in halo:
        copy.start()

    theirs = flip(my_k, 2)
    to_sibling = remote(raw.at[my_k], raw.at[my_k], kern_s.at[0], kern_r.at[0], sibling)
    to_across = remote(
        raw.at[my_k, 0], raw.at[my_k, 0], kern_s.at[1], kern_r.at[1], across
    )
    to_around = remote(
        raw.at[my_k, 1], raw.at[my_k, 1], kern_s.at[2], kern_r.at[2], around
    )
    onward = remote(raw.at[theirs], raw.at[theirs], kern_s.at[3], kern_r.at[3], sibling)
    to_across.start()
    to_around.start()
    to_sibling.start()

    sin, cos = sincos(window[...])
    row = lax.broadcasted_iota(jnp.int32, (2 * N, N), 0)
    keep = jnp.where(row < N, 1.0, 0.0)
    keep = jnp.where((row >= N) & (row < N + H) & (my_k < groups - 1), 1.0, keep)
    keep = jnp.where((row >= N + H) & (my_k > 0), 1.0, keep)
    trig[0] = cos * keep
    trig[1] = sin * keep

    def owner(j):
        low = jnp.where(lax.rem(j, 2) == 1, flip(my_k, 1), my_k)
        return jnp.where(j >= 2, flip(low, 2), low)

    def respond_cols(j):
        o = owner(j)
        even, odd = [], []
        edges = [raw[o, part, tall * count :] for part in range(2)]
        for n in range(count):
            pair = [[], []]
            for part in range(2):
                turned = raw[o, part, tall * n : tall * (n + 1)]
                extra = cat(
                    [
                        jnp.where(
                            lane == H, edges[part][:, count * g + n : count * g + n + 1], 0.0
                        )
                        for g in range(N // 8 + 1)
                    ],
                    0,
                )
                pair[0].append(turned + extra)
                pair[1].append(jnp.where(lane < H, turned, -turned) + extra)
            even.append(cat(pair[0], 1))
            odd.append(cat(pair[1], 1))
        return (
            right(cat(even, 0), fch[:, : 2 * N], fcl[:, : 2 * N]),
            right(cat(odd, 0), fch[:, 2 * N :], fcl[:, 2 * N :]),
        )

    def respond_rows(j, columns):
        o = owner(j)
        ge, go = columns
        row = lax.broadcasted_iota(jnp.int32, (N, 2 * N), 0)
        even, odd = [], []
        for n in range(count):
            pair = [[], []]
            at = slice(tall * n, tall * (n + 1))
            for c in (slice(0, N), slice(N, 2 * N)):
                g = cat([ge[at, c], go[at, c]], 1)
                extra = jnp.where(row == H, g[N : N + 1], 0.0)
                pair[0].append(cat([g[H:N], g[0:H]], 0) + extra)
                pair[1].append(cat([g[H:N], -g[0:H]], 0) + extra)
            even.append(cat(pair[0], 0))
            odd.append(cat(pair[1], 0))
        for p, x in enumerate((even, odd)):
            half = slice(2 * N * p, 2 * N * (p + 1))
            r = left(frh[half], frl[half], cat(x, 1))
            for n in range(count):
                resp[o, n, half] = r[:, 2 * N * n : 2 * N * (n + 1)]

    def field_rows(j):
        o = owner(j)
        xs = []
        for n in range(count):
            parts = []
            for p in range(2):
                low = slice(2 * N * p, 2 * N * p + N)
                high = slice(2 * N * p + N, 2 * N * (p + 1))
                rr, ri = resp[o, n, low], resp[o, n, high]
                sr, si = spec[low], spec[high]
                parts += [rr * sr - ri * si, rr * si + ri * sr]
            xs.append(cat(parts, 0))
        return left(fch[...], fcl[...], cat(xs, 1))

    def field_cols(j, z):
        o = owner(j)
        zs = []
        for n in range(count):
            q = z[:, 2 * N * n : 2 * N * (n + 1)]
            zs.append(cat([q[:N, :N], q[N:, :N], q[:N, N:], q[N:, N:]], 1))
        f = right(cat(zs, 0), frh[...], frl[...])
        field[o] = f
        q = f * f
        total = None
        for n in range(count):
            g = q[N * n : N * (n + 1)]
            term = g[:, :N] + g[:, N:]
            total = term if total is None else total + term
        return total

    respond_rows(0, respond_cols(0))

    for copy in halo:
        copy.wait_recv()
    first, last = my_s == 0, my_s == space - 1
    upper, lower = unpack(halo_in[0], halo_in[1])
    sin, cos = sincos(cat([upper, lower], 0))
    keep = jnp.where(lane < H, jnp.where(last, 0.0, 1.0), jnp.where(first, 0.0, 1.0)) * keep
    cos = cos * keep
    sin = sin * keep
    trig[2] = cos
    trig[3] = sin
    se = right(
        cat([trig[0] + cos, trig[1] + sin], 1), fch[:, : 2 * N], fcl[:, : 2 * N]
    )
    so = right(
        cat([trig[0] - cos, trig[1] - sin], 1), fch[:, 2 * N :], fcl[:, 2 * N :]
    )
    even, odd = [], []
    for c in (slice(0, N), slice(N, 2 * N)):
        g = cat([se[:, c], so[:, c]], 1)
        even.append(g[:N] + g[N:])
        odd.append(g[:N] - g[N:])
    spec[: 2 * N] = left(frh[: 2 * N], frl[: 2 * N], cat(even, 0))
    spec[2 * N :] = left(frh[2 * N :], frl[2 * N :], cat(odd, 0))

    def fields(j, total):
        @pl.when(j == 0)
        def _():
            to_sibling.wait_recv()

        @pl.when(j == 1)
        def _():
            to_across.wait_recv()
            to_around.wait_recv()
            onward.start()

        @pl.when(j == 2)
        def _():
            onward.wait_recv()

        columns = respond_cols(j + 1)
        z = field_rows(j)
        respond_rows(j + 1, columns)
        return total + field_cols(j, z)

    intensity = lax.fori_loop(0, groups - 1, fields, jnp.zeros((N, N), F32))
    intensity = intensity + field_cols(groups - 1, field_rows(groups - 1))

    resist = 1.0 / (1.0 + jnp.exp(-STEEP * (intensity - LEVEL)))
    resist_ref[...] = resist
    want = target_ref[pl.ds(own, N)].astype(F32)
    factor = 4.0 * STEEP * (resist - want) * resist * (1.0 - resist)

    def pull_cols(j):
        o = owner(j)
        xs = []
        for n in range(count):
            f = field[o, N * n : N * (n + 1)]
            xs.append(cat([factor * f[:, :N], factor * f[:, N:]], 1))
        yield_[lax.rem(j, 2)] = right(cat(xs, 0), fch[...], fcl[...])

    def pull_rows(j):
        o = owner(j)
        y = yield_[lax.rem(j, 2)]
        xs = []
        for n in range(count):
            q = y[N * n : N * (n + 1)]
            re = cat([q[:, :N], q[:, 2 * N : 3 * N]], 1)
            im = cat([q[:, N : 2 * N], q[:, 3 * N :]], 1)
            xs.append(cat([re, im], 0))
        v = left(frh[...], frl[...], cat(xs, 1))
        for p in range(2):
            low = slice(2 * N * p, 2 * N * p + N)
            high = slice(2 * N * p + N, 2 * N * (p + 1))
            re, im = acc[low], acc[high]
            for n in range(count):
                rr, ri = resp[o, n, low], resp[o, n, high]
                vr = v[low, 2 * N * n : 2 * N * (n + 1)]
                vi = v[high, 2 * N * n : 2 * N * (n + 1)]
                re = re + (rr * vr + ri * vi)
                im = im + (rr * vi - ri * vr)
            acc[low] = re
            acc[high] = im

    acc[...] = jnp.zeros((4 * N, 2 * N), F32)
    pull_cols(0)

    def pulls(j, carry):
        pull_cols(j + 1)
        pull_rows(j)
        return carry

    lax.fori_loop(0, groups - 1, pulls, 0)
    pull_rows(groups - 1)

    e = left(fch[:, : 2 * N], fcl[:, : 2 * N], acc[: 2 * N])
    o = left(fch[:, 2 * N :], fcl[:, 2 * N :], acc[2 * N :])
    u, v = e + o, e - o
    br = cat([u[:N], v[:N]], 0)
    bi = cat([u[N:], v[N:]], 0)
    e = right(cat([br[:, :N], bi[:, :N]], 1), frh[: 2 * N], frl[: 2 * N])
    o = right(cat([br[:, N:], bi[:, N:]], 1), frh[2 * N :], frl[2 * N :])
    u, v = e + o, e - o
    gout[0] = u[:, N:] * trig[0] - u[:, :N] * trig[1]
    side = v[:, N:] * trig[2] - v[:, :N] * trig[3]
    gout[1] = side
    pout[0], pout[1] = pack(side[:H], side[H:N])
    low_rows, high_rows = pl.ds(N, H), pl.ds(N + H, H)
    routes = [
        (gout.at[0, low_rows], (my_s, k_next)),
        (gout.at[0, high_rows], (my_s, k_prev)),
        (pout.at[0], (s_next, my_k)),
        (pout.at[1], (s_prev, my_k)),
        (gout.at[1, low_rows], (s_next, k_next)),
        (gout.at[1, low_rows], (s_prev, k_next)),
        (gout.at[1, high_rows], (s_next, k_prev)),
        (gout.at[1, high_rows], (s_prev, k_prev)),
    ]
    rims = [
        remote(src, rin.at[i], rim_s.at[i], rim_r.at[i], device)
        for i, (src, device) in enumerate(routes)
    ]
    for copy in rims:
        copy.start()
    for copy in rims:
        copy.wait_recv()
    has_low = jnp.where(lane < H, my_s, space - 1 - my_s) > 0
    upper, lower = unpack(rin[2], rin[3])
    upper = upper + jnp.where(my_k > 0, jnp.where(lane < H, rin[4], rin[5]), 0.0)
    lower = lower + jnp.where(my_k < groups - 1, jnp.where(lane < H, rin[6], rin[7]), 0.0)
    grad_ref[:H] = (
        gout[0, :H] + jnp.where(my_k > 0, rin[0], 0.0) + jnp.where(has_low, upper, 0.0)
    )
    grad_ref[H:] = (
        gout[0, H:N] + jnp.where(my_k < groups - 1, rin[1], 0.0) + jnp.where(has_low, lower, 0.0)
    )
    for copy in halo + rims + [to_sibling, to_across, to_around, onward]:
        copy.wait_send()


def body(space, groups, phase, target, kernels, weights):
    rows, cols = phase.shape
    count = kernels.shape[1]
    far = 8 if space % 16 == 0 else 1
    consts = [jnp.asarray(t) for t in tables()]
    vmem = pl.BlockSpec(memory_space=pltpu.VMEM)
    dma = pltpu.SemaphoreType.DMA
    return pl.pallas_call(
        functools.partial(kernel, space, groups, far),
        out_shape=[jax.ShapeDtypeStruct((N, cols), F32)] * 2,
        in_specs=[vmem, vmem, vmem, pl.BlockSpec(memory_space=pltpu.SMEM)] + [vmem] * 4,
        out_specs=[vmem, vmem],
        scratch_shapes=[
            pltpu.VMEM((2 * N, N), F32),
            pltpu.VMEM((2, N, N), F32),
            pltpu.VMEM((2, N, N), F32),
            pltpu.VMEM((4, 2 * N, N), F32),
            pltpu.VMEM((groups, 2, count * (N + 8) + 8, N), F32),
            pltpu.VMEM((groups, count, 4 * N, 2 * N), F32),
            pltpu.VMEM((4 * N, 2 * N), F32),
            pltpu.VMEM((groups, count * N, 2 * N), F32),
            pltpu.VMEM((4 * N, 2 * N), F32),
            pltpu.VMEM((2, count * N, 4 * N), F32),
            pltpu.VMEM((2, 2 * N, N), F32),
            pltpu.VMEM((2, H, N), F32),
            pltpu.VMEM((8, H, N), F32),
            dma((2,)), dma((2,)),
            dma((4,)), dma((4,)),
            dma((8,)), dma((8,)),
        ],
        compiler_params=pltpu.CompilerParams(
            collective_id=0, has_side_effects=True, vmem_limit_bytes=48 * 2**20
        ),
        cost_estimate=pl.CostEstimate(
            flops=14 * 10**9, bytes_accessed=4 * 10**6, transcendentals=0
        ),
        name="hopkins",
    )(phase, target, kernels, weights, *consts)


def solution(mesh):
    placed = (P(None, "space"), P(None, "space"), P(None, "kern", None, None), P("kern"))
    return jax.shard_map(
        functools.partial(body, mesh.shape["space"], mesh.shape["kern"]),
        mesh=mesh,
        in_specs=placed,
        out_specs=(P("kern", "space"), P("kern", "space")),
        check_vma=False,
    )
```

profile of v0, /device:TPU:1, one launch (start us, length us, event | category | flops | bytes accessed | tf_op | source)
XLA Modules:
  0.0 50.0 jit_solution(7152844943503984790)
XLA Ops:
  0.6 0.0 copy-start.3
  0.6 0.0 copy-start.4
  0.7 0.0 copy-start.5
  0.7 0.0 copy-start.6
  0.7 0.0 copy-start.2
  0.7 0.0 copy-start.1
  0.7 0.0 copy-start
  0.7 1.5 %copy.10.kern_ref = f32[2,4,129,129]{3,2,1,0:T(8,128)S(1)} copy(f32[2,4,129,129]{3,1,2,0:T(4,128)} %param.10) | data formatting | bytes 1065024 | tf_op args[2]
  2.3 0.0 copy-done.3
  2.3 0.0 copy-done.4
  2.3 0.0 copy-done.5
  2.3 0.0 copy-done.6
  2.3 0.0 copy-done.2
  2.3 0.0 copy-done.1
  2.3 0.0 copy-done
  2.3 46.4 %hopkins.1 = (f32[128,128]{1,0:T(8,128)S(1)}, f32[128,128]{1,0:T(8,128)S(1)}) custom-call(f32[512,128]{1,0:T(8,128)S(1)} %copy-done, s32[512,128]{1,0:T(8,128)S(1)} %copy-done.1, f32[2,4,129,129]{3,2,1,0:T(8,128)S(1)} %copy.10.kern_ref, f32[4]{0:T(128)S(1)} %copy-done.2, bf16[256,512]{1,0:T(8,128)(2,1)S(1)} %copy-done.6, bf16[256,512]{1,0:T(8,128)(2,1)S(1)} %copy-done.5, ...), custom_call_target="tpu_custom_call" | custom-call | flops 14000000000 | bytes 4000000 | tf_op jit(solution)/shard_map/hopkins/pallas_call | solution.py:408
  48.8 0.6 %copy.13 = f32[128,128]{1,0:T(8,128)} copy(f32[128,128]{1,0:T(8,128)S(1)} %get-tuple-element.4) | data formatting | bytes 131072
  49.4 0.6 %copy.14 = f32[128,128]{1,0:T(8,128)} copy(f32[128,128]{1,0:T(8,128)S(1)} %get-tuple-element.5) | data formatting | bytes 131072
Async XLA Ops:
  0.6 1.6 %copy-start.3 = (bf16[512,256]{1,0:T(8,128)(2,1)S(1)}, bf16[512,256]{1,0:T(8,128)(2,1)}, u32[]{:S(2)}) copy-start(bf16[512,256]{1,0:T(8,128)(2,1)} %constant.11.clone.frl) | copy-start | bytes 786436
  0.6 1.6 %copy-start.4 = (bf16[512,256]{1,0:T(8,128)(2,1)S(1)}, bf16[512,256]{1,0:T(8,128)(2,1)}, u32[]{:S(2)}) copy-start(bf16[512,256]{1,0:T(8,128)(2,1)} %constant.10.clone.frh) | copy-start | bytes 786436
  0.7 1.6 %copy-start.5 = (bf16[256,512]{1,0:T(8,128)(2,1)S(1)}, bf16[256,512]{1,0:T(8,128)(2,1)}, u32[]{:S(2)}) copy-start(bf16[256,512]{1,0:T(8,128)(2,1)} %constant.9.clone.fcl) | copy-start | bytes 786436
  0.7 1.6 %copy-start.6 = (bf16[256,512]{1,0:T(8,128)(2,1)S(1)}, bf16[256,512]{1,0:T(8,128)(2,1)}, u32[]{:S(2)}) copy-start(bf16[256,512]{1,0:T(8,128)(2,1)} %constant.8.clone.fch) | copy-start | bytes 786436
  0.7 1.6 %copy-start.2 = (f32[4]{0:T(128)S(1)}, f32[4]{0:T(128)}, u32[]{:S(2)}) copy-start(f32[4]{0:T(128)} %weight_ref.1) | copy-start | bytes 52
  0.7 1.6 %copy-start.1 = (s32[512,128]{1,0:T(8,128)S(1)}, s32[512,128]{1,0:T(8,128)}, u32[]{:S(2)}) copy-start(s32[512,128]{1,0:T(8,128)} %target_ref.1) | copy-start | bytes 786436
  0.7 1.6 %copy-start = (f32[512,128]{1,0:T(8,128)S(1)}, f32[512,128]{1,0:T(8,128)}, u32[]{:S(2)}) copy-start(f32[512,128]{1,0:T(8,128)} %phase_ref.1) | copy-start | bytes 786436
where the time goes:
time: 50.1 us; the launch traced here: 50 us
  Pallas kernels  46.4 us (93%)
  local copies, waits for them, and re-layouts  2.85 us (6%)
  between operations  0.75 us (1%)
    pallas_call x1, Pallas kernels, body(): pl.pallas_call(functools.partial(kernel, space, groups, far), out_shape=[...  46.4 us
    unnamed x17, local copies, waits for them, and re-layouts  2.85 us

commit v1 on v0

--- a/solution.py
+++ b/solution.py
@@ -81,7 +81,7 @@
     space, groups, far,
     phase_ref, target_ref, kern_ref, weight_ref, fch, fcl, frh, frl,
     resist_ref, grad_ref,
-    window, halo_out, halo_in, trig, raw, resp, spec, field, acc, yield_, gout, pout, rin,
+    window, halo_out, halo_in, trig, raw, resp, spec, field, acc, gout, pout, rin,
     halo_s, halo_r, kern_s, kern_r, rim_s, rim_r,
 ):
     rows = phase_ref.shape[0]
@@ -97,13 +97,33 @@
     across = (my_s, flip(my_k, 2))
     around = (flip(my_s, far), flip(my_k, 2))
 
+    mirror = (my_s, flip(flip(my_k, 1), 2))
+    has_next, has_prev = my_s < space - 1, my_s > 0
+    up, down = my_k < groups - 1, my_k > 0
+
     barrier = pltpu.get_barrier_semaphore()
     greeted = [
-        (s_next, my_k), (s_prev, my_k), sibling, across, (my_s, flip(flip(my_k, 1), 2)), around,
-        (s_next, k_next), (s_next, k_prev), (s_prev, k_next), (s_prev, k_prev),
+        (sibling, None), (across, None), (around, None), (mirror, up & down),
+        ((s_next, my_k), has_next), ((s_prev, my_k), has_prev),
+        ((s_next, k_next), has_next & up), ((s_next, k_prev), has_next & down),
+        ((s_prev, k_next), has_prev & up), ((s_prev, k_prev), has_prev & down),
     ]
-    for device in greeted:
-        pl.semaphore_signal(barrier, inc=1, device_id=device, device_id_type=MESH)
+
+    def when(condition, action):
+        if condition is None:
+            action()
+        else:
+            pl.when(condition)(action)
+
+    expected = 0
+    for device, condition in greeted:
+        when(
+            condition,
+            functools.partial(
+                pl.semaphore_signal, barrier, inc=1, device_id=device, device_id_type=MESH
+            ),
+        )
+        expected = expected + (1 if condition is None else jnp.where(condition, 1, 0))
 
     lane = lax.broadcasted_iota(jnp.int32, (8, N), 1)[:1]
 
@@ -140,48 +160,42 @@
         edges = jnp.zeros((8, N), F32)
         for n in range(count):
             gain = gains[n]
-            raw[my_k, part, tall * n : tall * n + N] = (
+            raw[0, part, tall * n : tall * n + N] = (
                 pltpu.roll(kern_ref[part, n, 0:N, 0:N], H, 1) * gain
             )
             last = jnp.broadcast_to(kern_ref[part, n, N : N + 1, 0:N], (8, N))
-            raw[my_k, part, tall * n + N : tall * (n + 1)] = pltpu.roll(last, H, 1) * gain
+            raw[0, part, tall * n + N : tall * (n + 1)] = pltpu.roll(last, H, 1) * gain
             for g in range(N // 8 + 1):
                 end = 8 * g + 8 if g < N // 8 else N + 1
                 column = kern_ref[part, n, 8 * g : end, N : N + 1]
                 edges = jnp.where(lane == count * g + n, column * gain, edges)
-        raw[my_k, part, tall * count :] = edges
-
-    pl.semaphore_wait(barrier, len(greeted))
-    for copy in halo:
-        copy.start()
+        raw[0, part, tall * count :] = edges
+
+    pl.semaphore_wait(barrier, expected)
+    when(has_prev, halo[0].start)
+    when(has_next, halo[1].start)
 
     theirs = flip(my_k, 2)
-    to_sibling = remote(raw.at[my_k], raw.at[my_k], kern_s.at[0], kern_r.at[0], sibling)
-    to_across = remote(
-        raw.at[my_k, 0], raw.at[my_k, 0], kern_s.at[1], kern_r.at[1], across
-    )
-    to_around = remote(
-        raw.at[my_k, 1], raw.at[my_k, 1], kern_s.at[2], kern_r.at[2], around
-    )
-    onward = remote(raw.at[theirs], raw.at[theirs], kern_s.at[3], kern_r.at[3], sibling)
+    to_across = remote(raw.at[0, 0], raw.at[1, 0], kern_s.at[0], kern_r.at[0], across)
+    to_around = remote(raw.at[0, 1], raw.at[1, 1], kern_s.at[1], kern_r.at[1], around)
     to_across.start()
     to_around.start()
-    to_sibling.start()
+
+    def shared(group, parity, index):
+        half = resp.at[group, :, pl.ds(2 * N * parity, 2 * N)]
+        return remote(half, half, kern_s.at[index], kern_r.at[index], sibling)
+
+    first_group = [shared(my_k, 0, 2), shared(my_k, 1, 3)]
+    second_group = [shared(theirs, 0, 4), shared(theirs, 1, 5)]
 
     sin, cos = sincos(window[...])
     row = lax.broadcasted_iota(jnp.int32, (2 * N, N), 0)
-    keep = jnp.where(row < N, 1.0, 0.0)
-    keep = jnp.where((row >= N) & (row < N + H) & (my_k < groups - 1), 1.0, keep)
-    keep = jnp.where((row >= N + H) & (my_k > 0), 1.0, keep)
-    trig[0] = cos * keep
-    trig[1] = sin * keep
-
-    def owner(j):
-        low = jnp.where(lax.rem(j, 2) == 1, flip(my_k, 1), my_k)
-        return jnp.where(j >= 2, flip(low, 2), low)
-
-    def respond_cols(j):
-        o = owner(j)
+    missing = jnp.where((row >= N) & (row < N + H) & (my_k == groups - 1), 1, 0)
+    missing = jnp.where((row >= N + H) & (my_k == 0), 1, missing)
+    trig[0] = jnp.where(missing == 0, cos, 0.0)
+    trig[1] = jnp.where(missing == 0, sin, 0.0)
+
+    def respond_cols(o):
         even, odd = [], []
         edges = [raw[o, part, tall * count :] for part in range(2)]
         for n in range(count):
@@ -206,8 +220,7 @@
             right(cat(odd, 0), fch[:, 2 * N :], fcl[:, 2 * N :]),
         )
 
-    def respond_rows(j, columns):
-        o = owner(j)
+    def respond_rows(o, columns, copies):
         ge, go = columns
         row = lax.broadcasted_iota(jnp.int32, (N, 2 * N), 0)
         even, odd = [], []
@@ -226,11 +239,14 @@
             r = left(frh[half], frl[half], cat(x, 1))
             for n in range(count):
                 resp[o, n, half] = r[:, 2 * N * n : 2 * N * (n + 1)]
-
-    def field_rows(j):
-        o = owner(j)
+            copies[p].start()
+
+    def members(owners):
+        return [(o, n) for o in owners for n in range(count)]
+
+    def field_rows(owners):
         xs = []
-        for n in range(count):
+        for o, n in members(owners):
             parts = []
             for p in range(2):
                 low = slice(2 * N * p, 2 * N * p + N)
@@ -241,32 +257,32 @@
             xs.append(cat(parts, 0))
         return left(fch[...], fcl[...], cat(xs, 1))
 
-    def field_cols(j, z):
-        o = owner(j)
+    def fields(owners):
+        z = field_rows(owners)
         zs = []
-        for n in range(count):
+        for n in range(len(owners) * count):
             q = z[:, 2 * N * n : 2 * N * (n + 1)]
             zs.append(cat([q[:N, :N], q[N:, :N], q[:N, N:], q[N:, N:]], 1))
         f = right(cat(zs, 0), frh[...], frl[...])
-        field[o] = f
+        for i, o in enumerate(owners):
+            field[o] = f[N * count * i : N * count * (i + 1)]
         q = f * f
         total = None
-        for n in range(count):
+        for n in range(len(owners) * count):
             g = q[N * n : N * (n + 1)]
             term = g[:, :N] + g[:, N:]
             total = term if total is None else total + term
         return total
 
-    respond_rows(0, respond_cols(0))
-
-    for copy in halo:
-        copy.wait_recv()
-    first, last = my_s == 0, my_s == space - 1
+    respond_rows(my_k, respond_cols(0), first_group)
+
+    when(has_next, halo[0].wait_recv)
+    when(has_prev, halo[1].wait_recv)
     upper, lower = unpack(halo_in[0], halo_in[1])
     sin, cos = sincos(cat([upper, lower], 0))
-    keep = jnp.where(lane < H, jnp.where(last, 0.0, 1.0), jnp.where(first, 0.0, 1.0)) * keep
-    cos = cos * keep
-    sin = sin * keep
+    inside = jnp.where(lane < H, space - 1 - my_s, my_s) > 0
+    cos = jnp.where(inside & (missing == 0), cos, 0.0)
+    sin = jnp.where(inside & (missing == 0), sin, 0.0)
     trig[2] = cos
     trig[3] = sin
     se = right(
@@ -283,48 +299,32 @@
     spec[: 2 * N] = left(frh[: 2 * N], frl[: 2 * N], cat(even, 0))
     spec[2 * N :] = left(frh[2 * N :], frl[2 * N :], cat(odd, 0))
 
-    def fields(j, total):
-        @pl.when(j == 0)
-        def _():
-            to_sibling.wait_recv()
-
-        @pl.when(j == 1)
-        def _():
-            to_across.wait_recv()
-            to_around.wait_recv()
-            onward.start()
-
-        @pl.when(j == 2)
-        def _():
-            onward.wait_recv()
-
-        columns = respond_cols(j + 1)
-        z = field_rows(j)
-        respond_rows(j + 1, columns)
-        return total + field_cols(j, z)
-
-    intensity = lax.fori_loop(0, groups - 1, fields, jnp.zeros((N, N), F32))
-    intensity = intensity + field_cols(groups - 1, field_rows(groups - 1))
+    kin, theirs_kin = flip(my_k, 1), flip(theirs, 1)
+    for copy in first_group:
+        copy.wait_recv()
+    intensity = fields((my_k, kin))
+    to_across.wait_recv()
+    to_around.wait_recv()
+    respond_rows(theirs, respond_cols(1), second_group)
+    intensity = intensity + fields((theirs,))
+    for copy in second_group:
+        copy.wait_recv()
+    intensity = intensity + fields((theirs_kin,))
 
     resist = 1.0 / (1.0 + jnp.exp(-STEEP * (intensity - LEVEL)))
     resist_ref[...] = resist
     want = target_ref[pl.ds(own, N)].astype(F32)
     factor = 4.0 * STEEP * (resist - want) * resist * (1.0 - resist)
 
-    def pull_cols(j):
-        o = owner(j)
+    def pulls(owners):
         xs = []
-        for n in range(count):
+        for o, n in members(owners):
             f = field[o, N * n : N * (n + 1)]
             xs.append(cat([factor * f[:, :N], factor * f[:, N:]], 1))
-        yield_[lax.rem(j, 2)] = right(cat(xs, 0), fch[...], fcl[...])
-
-    def pull_rows(j):
-        o = owner(j)
-        y = yield_[lax.rem(j, 2)]
+        y = right(cat(xs, 0), fch[...], fcl[...])
         xs = []
-        for n in range(count):
-            q = y[N * n : N * (n + 1)]
+        for i in range(len(owners) * count):
+            q = y[N * i : N * (i + 1)]
             re = cat([q[:, :N], q[:, 2 * N : 3 * N]], 1)
             im = cat([q[:, N : 2 * N], q[:, 3 * N :]], 1)
             xs.append(cat([re, im], 0))
@@ -333,25 +333,23 @@
             low = slice(2 * N * p, 2 * N * p + N)
             high = slice(2 * N * p + N, 2 * N * (p + 1))
             re, im = acc[low], acc[high]
-            for n in range(count):
+            for i, (o, n) in enumerate(members(owners)):
                 rr, ri = resp[o, n, low], resp[o, n, high]
-                vr = v[low, 2 * N * n : 2 * N * (n + 1)]
-                vi = v[high, 2 * N * n : 2 * N * (n + 1)]
+                vr = v[low, 2 * N * i : 2 * N * (i + 1)]
+                vi = v[high, 2 * N * i : 2 * N * (i + 1)]
                 re = re + (rr * vr + ri * vi)
                 im = im + (rr * vi - ri * vr)
             acc[low] = re
             acc[high] = im
 
     acc[...] = jnp.zeros((4 * N, 2 * N), F32)
-    pull_cols(0)
-
-    def pulls(j, carry):
-        pull_cols(j + 1)
-        pull_rows(j)
+
+    def pull_step(j, carry):
+        low = jnp.where(j == 0, my_k, theirs)
+        pulls((low, flip(low, 1)))
         return carry
 
-    lax.fori_loop(0, groups - 1, pulls, 0)
-    pull_rows(groups - 1)
+    lax.fori_loop(0, 2, pull_step, 0)
 
     e = left(fch[:, : 2 * N], fcl[:, : 2 * N], acc[: 2 * N])
     o = left(fch[:, 2 * N :], fcl[:, 2 * N :], acc[2 * N :])
@@ -367,23 +365,23 @@
     pout[0], pout[1] = pack(side[:H], side[H:N])
     low_rows, high_rows = pl.ds(N, H), pl.ds(N + H, H)
     routes = [
-        (gout.at[0, low_rows], (my_s, k_next)),
-        (gout.at[0, high_rows], (my_s, k_prev)),
-        (pout.at[0], (s_next, my_k)),
-        (pout.at[1], (s_prev, my_k)),
-        (gout.at[1, low_rows], (s_next, k_next)),
-        (gout.at[1, low_rows], (s_prev, k_next)),
-        (gout.at[1, high_rows], (s_next, k_prev)),
-        (gout.at[1, high_rows], (s_prev, k_prev)),
+        (gout.at[0, low_rows], (my_s, k_next), up, down),
+        (gout.at[0, high_rows], (my_s, k_prev), down, up),
+        (pout.at[0], (s_next, my_k), has_next, has_prev),
+        (pout.at[1], (s_prev, my_k), has_prev, has_next),
+        (gout.at[1, low_rows], (s_next, k_next), has_next & up, has_prev & down),
+        (gout.at[1, low_rows], (s_prev, k_next), has_prev & up, has_next & down),
+        (gout.at[1, high_rows], (s_next, k_prev), has_next & down, has_prev & up),
+        (gout.at[1, high_rows], (s_prev, k_prev), has_prev & down, has_next & up),
     ]
     rims = [
         remote(src, rin.at[i], rim_s.at[i], rim_r.at[i], device)
-        for i, (src, device) in enumerate(routes)
+        for i, (src, device, _, _) in enumerate(routes)
     ]
-    for copy in rims:
-        copy.start()
-    for copy in rims:
-        copy.wait_recv()
+    for i in (4, 5, 6, 7, 2, 3, 0, 1):
+        when(routes[i][2], rims[i].start)
+    for i in range(8):
+        when(routes[i][3], rims[i].wait_recv)
     has_low = jnp.where(lane < H, my_s, space - 1 - my_s) > 0
     upper, lower = unpack(rin[2], rin[3])
     upper = upper + jnp.where(my_k > 0, jnp.where(lane < H, rin[4], rin[5]), 0.0)
@@ -394,8 +392,12 @@
     grad_ref[H:] = (
         gout[0, H:N] + jnp.where(my_k < groups - 1, rin[1], 0.0) + jnp.where(has_low, lower, 0.0)
     )
-    for copy in halo + rims + [to_sibling, to_across, to_around, onward]:
+    when(has_prev, halo[0].wait_send)
+    when(has_next, halo[1].wait_send)
+    for copy in [to_across, to_around] + first_group + second_group:
         copy.wait_send()
+    for i in range(8):
+        when(routes[i][2], rims[i].wait_send)
 
 
 def body(space, groups, phase, target, kernels, weights):
@@ -415,17 +417,16 @@
             pltpu.VMEM((2, N, N), F32),
             pltpu.VMEM((2, N, N), F32),
             pltpu.VMEM((4, 2 * N, N), F32),
-            pltpu.VMEM((groups, 2, count * (N + 8) + 8, N), F32),
+            pltpu.VMEM((2, 2, count * (N + 8) + 8, N), F32),
             pltpu.VMEM((groups, count, 4 * N, 2 * N), F32),
             pltpu.VMEM((4 * N, 2 * N), F32),
             pltpu.VMEM((groups, count * N, 2 * N), F32),
             pltpu.VMEM((4 * N, 2 * N), F32),
-            pltpu.VMEM((2, count * N, 4 * N), F32),
             pltpu.VMEM((2, 2 * N, N), F32),
             pltpu.VMEM((2, H, N), F32),
             pltpu.VMEM((8, H, N), F32),
             dma((2,)), dma((2,)),
-            dma((4,)), dma((4,)),
+            dma((6,)), dma((6,)),
             dma((8,)), dma((8,)),
         ],
         compiler_params=pltpu.CompilerParams(

time: 50.1 us -> 45 us (0.90)
  the two profiles are of different devices: /device:TPU:1 before, /device:TPU:7 now
where the time goes in v1:
time: 45 us; the launch traced here: 44.9 us
  Pallas kernels  41.3 us (92%)
  local copies, waits for them, and re-layouts  2.85 us (6%)
  between operations  0.75 us (2%)
    pallas_call x1, Pallas kernels, body(): pl.pallas_call(functools.partial(kernel, space, groups, far), out_shape=[...  41.3 us
    unnamed x17, local copies, waits for them, and re-layouts  2.85 us

profile of v1, /device:TPU:7, one launch (start us, length us, event | category | flops | bytes accessed | tf_op | source)
XLA Modules:
  0.0 44.9 jit_solution(13368546429392472590)
XLA Ops:
  0.6 0.0 copy-start.3
  0.6 0.0 copy-start.4
  0.7 0.0 copy-start.5
  0.7 0.0 copy-start.6
  0.7 0.0 copy-start.2
  0.7 0.0 copy-start.1
  0.7 0.0 copy-start
  0.7 1.5 %copy.10.kern_ref = f32[2,4,129,129]{3,2,1,0:T(8,128)S(1)} copy(f32[2,4,129,129]{3,1,2,0:T(4,128)} %param.10) | data formatting | bytes 1065024 | tf_op args[2]
  2.3 0.0 copy-done.3
  2.3 0.0 copy-done.4
  2.3 0.0 copy-done.5
  2.3 0.0 copy-done.6
  2.3 0.0 copy-done.2
  2.3 0.0 copy-done.1
  2.3 0.0 copy-done
  2.3 41.3 %hopkins.1 = (f32[128,128]{1,0:T(8,128)S(1)}, f32[128,128]{1,0:T(8,128)S(1)}) custom-call(f32[512,128]{1,0:T(8,128)S(1)} %copy-done, s32[512,128]{1,0:T(8,128)S(1)} %copy-done.1, f32[2,4,129,129]{3,2,1,0:T(8,128)S(1)} %copy.10.kern_ref, f32[4]{0:T(128)S(1)} %copy-done.2, bf16[256,512]{1,0:T(8,128)(2,1)S(1)} %copy-done.6, bf16[256,512]{1,0:T(8,128)(2,1)S(1)} %copy-done.5, ...), custom_call_target="tpu_custom_call" | custom-call | flops 14000000000 | bytes 4000000 | tf_op jit(solution)/shard_map/hopkins/pallas_call | solution.py:410
  43.7 0.6 %copy.13 = f32[128,128]{1,0:T(8,128)} copy(f32[128,128]{1,0:T(8,128)S(1)} %get-tuple-element.4) | data formatting | bytes 131072
  44.3 0.6 %copy.14 = f32[128,128]{1,0:T(8,128)} copy(f32[128,128]{1,0:T(8,128)S(1)} %get-tuple-element.5) | data formatting | bytes 131072
Async XLA Ops:
  0.6 1.6 %copy-start.3 = (bf16[512,256]{1,0:T(8,128)(2,1)S(1)}, bf16[512,256]{1,0:T(8,128)(2,1)}, u32[]{:S(2)}) copy-start(bf16[512,256]{1,0:T(8,128)(2,1)} %constant.11.clone.frl) | copy-start | bytes 786436
  0.6 1.6 %copy-start.4 = (bf16[512,256]{1,0:T(8,128)(2,1)S(1)}, bf16[512,256]{1,0:T(8,128)(2,1)}, u32[]{:S(2)}) copy-start(bf16[512,256]{1,0:T(8,128)(2,1)} %constant.10.clone.frh) | copy-start | bytes 786436
  0.7 1.6 %copy-start.5 = (bf16[256,512]{1,0:T(8,128)(2,1)S(1)}, bf16[256,512]{1,0:T(8,128)(2,1)}, u32[]{:S(2)}) copy-start(bf16[256,512]{1,0:T(8,128)(2,1)} %constant.9.clone.fcl) | copy-start | bytes 786436
  0.7 1.6 %copy-start.6 = (bf16[256,512]{1,0:T(8,128)(2,1)S(1)}, bf16[256,512]{1,0:T(8,128)(2,1)}, u32[]{:S(2)}) copy-start(bf16[256,512]{1,0:T(8,128)(2,1)} %constant.8.clone.fch) | copy-start | bytes 786436
  0.7 1.6 %copy-start.2 = (f32[4]{0:T(128)S(1)}, f32[4]{0:T(128)}, u32[]{:S(2)}) copy-start(f32[4]{0:T(128)} %weight_ref.1) | copy-start | bytes 52
  0.7 1.6 %copy-start.1 = (s32[512,128]{1,0:T(8,128)S(1)}, s32[512,128]{1,0:T(8,128)}, u32[]{:S(2)}) copy-start(s32[512,128]{1,0:T(8,128)} %target_ref.1) | copy-start | bytes 786436
  0.7 1.6 %copy-start = (f32[512,128]{1,0:T(8,128)S(1)}, f32[512,128]{1,0:T(8,128)}, u32[]{:S(2)}) copy-start(f32[512,128]{1,0:T(8,128)} %phase_ref.1) | copy-start | bytes 786436

commit v2 on v1

--- a/solution.py
+++ b/solution.py
@@ -79,16 +79,29 @@
 
 def kernel(
     space, groups, far,
-    phase_ref, target_ref, kern_ref, weight_ref, fch, fcl, frh, frl,
+    phase_hbm, target_hbm, kern_hbm, weight_ref, fch_hbm, fcl_hbm, frh_hbm, frl_hbm,
     resist_ref, grad_ref,
+    phase_ref, target_ref, kern_ref, fch, fcl, frh, frl, load_s,
     window, halo_out, halo_in, trig, raw, resp, spec, field, acc, gout, pout, rin,
     halo_s, halo_r, kern_s, kern_r, rim_s, rim_r,
 ):
-    rows = phase_ref.shape[0]
-    count = kern_ref.shape[1]
+    rows = phase_hbm.shape[0]
+    count = kern_hbm.shape[2]
+    my_k = lax.axis_index("kern")
+    own = pl.multiple_of(my_k * N, N)
+    pairs = [(phase_hbm, phase_ref)]
+    pairs += [
+        (kern_hbm.at[part, :, n], kern_ref.at[part, n]) for part in range(2) for n in range(count)
+    ]
+    pairs += [(fch_hbm, fch), (fcl_hbm, fcl), (frh_hbm, frh), (frl_hbm, frl)]
+    pairs += [(target_hbm.at[pl.ds(own, N)], target_ref)]
+    loads = [
+        pltpu.make_async_copy(src, dst, load_s.at[i]) for i, (src, dst) in enumerate(pairs)
+    ]
+    for load in loads:
+        load.start()
     tall = N + 8
     my_s = lax.axis_index("space")
-    my_k = lax.axis_index("kern")
     s_next = lax.rem(my_s + 1, space)
     s_prev = lax.rem(my_s + space - 1, space)
     k_next = lax.rem(my_k + 1, groups)
@@ -141,7 +154,7 @@
             device_id=device, device_id_type=MESH,
         )
 
-    own = pl.multiple_of(my_k * N, N)
+    loads[0].wait()
     after = pl.multiple_of(jnp.minimum(own + N, rows - H), H)
     before = pl.multiple_of(jnp.maximum(own - H, 0), H)
     window[0:N] = phase_ref[pl.ds(own, N)]
@@ -153,6 +166,8 @@
         remote(halo_out.at[1], halo_in.at[1], halo_s.at[1], halo_r.at[1], (s_next, my_k)),
     ]
 
+    for load in loads[1 : 1 + 2 * count]:
+        load.wait()
     gains = [
         jnp.sqrt(jnp.zeros((1, N), F32) + weight_ref[n]) * 2.0**-16 for n in range(count)
     ]
@@ -274,7 +289,12 @@
             total = term if total is None else total + term
         return total
 
+    for load in loads[1 + 2 * count :]:
+        load.wait()
     respond_rows(my_k, respond_cols(0), first_group)
+    to_across.wait_recv()
+    to_around.wait_recv()
+    respond_rows(theirs, respond_cols(1), second_group)
 
     when(has_next, halo[0].wait_recv)
     when(has_prev, halo[1].wait_recv)
@@ -303,9 +323,6 @@
     for copy in first_group:
         copy.wait_recv()
     intensity = fields((my_k, kin))
-    to_across.wait_recv()
-    to_around.wait_recv()
-    respond_rows(theirs, respond_cols(1), second_group)
     intensity = intensity + fields((theirs,))
     for copy in second_group:
         copy.wait_recv()
@@ -313,7 +330,7 @@
 
     resist = 1.0 / (1.0 + jnp.exp(-STEEP * (intensity - LEVEL)))
     resist_ref[...] = resist
-    want = target_ref[pl.ds(own, N)].astype(F32)
+    want = target_ref[...].astype(F32)
     factor = 4.0 * STEEP * (resist - want) * resist * (1.0 - resist)
 
     def pulls(owners):
@@ -406,13 +423,21 @@
     far = 8 if space % 16 == 0 else 1
     consts = [jnp.asarray(t) for t in tables()]
     vmem = pl.BlockSpec(memory_space=pltpu.VMEM)
+    hbm = pl.BlockSpec(memory_space=pltpu.HBM)
     dma = pltpu.SemaphoreType.DMA
     return pl.pallas_call(
         functools.partial(kernel, space, groups, far),
         out_shape=[jax.ShapeDtypeStruct((N, cols), F32)] * 2,
-        in_specs=[vmem, vmem, vmem, pl.BlockSpec(memory_space=pltpu.SMEM)] + [vmem] * 4,
+        in_specs=[hbm] * 3 + [pl.BlockSpec(memory_space=pltpu.SMEM)] + [hbm] * 4,
         out_specs=[vmem, vmem],
         scratch_shapes=[
+            pltpu.VMEM((rows, N), F32),
+            pltpu.VMEM((N, N), jnp.int32),
+            pltpu.VMEM((2, count, N + 1, N + 1), F32),
+        ]
+        + [pltpu.VMEM(t.shape, BF16) for t in consts]
+        + [
+            dma((6 + 2 * count,)),
             pltpu.VMEM((2 * N, N), F32),
             pltpu.VMEM((2, N, N), F32),
             pltpu.VMEM((2, N, N), F32),
@@ -430,13 +455,13 @@
             dma((8,)), dma((8,)),
         ],
         compiler_params=pltpu.CompilerParams(
-            collective_id=0, has_side_effects=True, vmem_limit_bytes=48 * 2**20
+            collective_id=0, has_side_effects=True, vmem_limit_bytes=int(53.8 * 2**20)
         ),
         cost_estimate=pl.CostEstimate(
             flops=14 * 10**9, bytes_accessed=4 * 10**6, transcendentals=0
         ),
         name="hopkins",
-    )(phase, target, kernels, weights, *consts)
+    )(phase, target, jnp.transpose(kernels, (0, 2, 1, 3)), weights, *consts)
 
 
 def solution(mesh):

time: 45 us -> 43 us (0.956)
  Pallas kernels: 41.3 us -> 40.1 us
  local copies, waits for them, and re-layouts: 2.85 us -> 1.91 us
    pallas_call x1, Pallas kernels: 41.3 us -> 40.1 us  [body(): pl.pallas_call(functools.partial(kernel, space, groups, far), out_shape=[...]
    unnamed x17 -> x4, local copies, waits for them, and re-layouts: 2.85 us -> 1.91 us
where the time goes in v2:
time: 43 us; the launch traced here: 42.7 us
  Pallas kernels  40.1 us (93%)
  local copies, waits for them, and re-layouts  1.91 us (4%)
  between operations  0.65 us (2%)
    pallas_call x1, Pallas kernels, body(): pl.pallas_call(functools.partial(kernel, space, groups, far), out_shape=[...  40.1 us
    unnamed x4, local copies, waits for them, and re-layouts  1.91 us

profile of v2, /device:TPU:7, one launch (start us, length us, event | category | flops | bytes accessed | tf_op | source)
XLA Modules:
  0.0 42.7 jit_solution(987618141140494523)
XLA Ops:
  0.6 0.0 copy-start
  0.6 0.6 %copy-done = f32[4]{0:T(128)S(1)} copy-done((f32[4]{0:T(128)S(1)}, f32[4]{0:T(128)}, u32[]{:S(2)}) %copy-start) | copy-done | bytes 40
  1.3 40.1 %hopkins.1 = (f32[128,128]{1,0:T(8,128)S(1)}, f32[128,128]{1,0:T(8,128)S(1)}) custom-call(f32[512,128]{1,0:T(8,128)} %phase_hbm.1, s32[512,128]{1,0:T(8,128)} %target_hbm.1, f32[2,129,4,129]{3,2,1,0:T(4,128)} %bitcast.1, f32[4]{0:T(128)S(1)} %copy-done, bf16[256,512]{1,0:T(8,128)(2,1)} %constant.8.clone.fch_hbm, bf16[256,512]{1,0:T(8,128)(2,1)} %constant.9.clone.fcl_hbm, ...), custom_call_target="tpu_custom_call" | custom-call | flops 14000000000 | bytes 4000000 | tf_op jit(solution)/shard_map/hopkins/pallas_call | solution.py:428
  41.4 0.6 %copy.12 = f32[128,128]{1,0:T(8,128)} copy(f32[128,128]{1,0:T(8,128)S(1)} %get-tuple-element.4) | data formatting | bytes 131072
  42.1 0.6 %copy.13 = f32[128,128]{1,0:T(8,128)} copy(f32[128,128]{1,0:T(8,128)S(1)} %get-tuple-element.5) | data formatting | bytes 131072
Async XLA Ops:
  0.6 0.7 %copy-start = (f32[4]{0:T(128)S(1)}, f32[4]{0:T(128)}, u32[]{:S(2)}) copy-start(f32[4]{0:T(128)} %weight_ref.1) | copy-start | bytes 52

commit v3 on v2

--- a/solution.py
+++ b/solution.py
@@ -82,7 +82,7 @@
     phase_hbm, target_hbm, kern_hbm, weight_ref, fch_hbm, fcl_hbm, frh_hbm, frl_hbm,
     resist_ref, grad_ref,
     phase_ref, target_ref, kern_ref, fch, fcl, frh, frl, load_s,
-    window, halo_out, halo_in, trig, raw, resp, spec, field, acc, gout, pout, rin,
+    window, halo_out, halo_in, trig, raw, resp, spec, field, acc, gout, pout, cout, rin, cin,
     halo_s, halo_r, kern_s, kern_r, rim_s, rim_r,
 ):
     rows = phase_hbm.shape[0]
@@ -127,6 +127,8 @@
             action()
         else:
             pl.when(condition)(action)
+
+    stage = pl.when(my_s >= 0)
 
     expected = 0
     for device, condition in greeted:
@@ -196,12 +198,20 @@
     to_across.start()
     to_around.start()
 
-    def shared(group, parity, index):
-        half = resp.at[group, :, pl.ds(2 * N * parity, 2 * N)]
+    def shared(group, number, parity, index):
+        half = resp.at[group, pl.ds(0, number), pl.ds(2 * N * parity, 2 * N)]
         return remote(half, half, kern_s.at[index], kern_r.at[index], sibling)
 
-    first_group = [shared(my_k, 0, 2), shared(my_k, 1, 3)]
-    second_group = [shared(theirs, 0, 4), shared(theirs, 1, 5)]
+    def passed(part, index):
+        span = pl.ds(tall * (count // 2), tall * (count - count // 2) + 8)
+        return remote(
+            raw.at[1, part, span], raw.at[2, part, span],
+            kern_s.at[index], kern_r.at[index], sibling,
+        )
+
+    first_group = [shared(my_k, count, 0, 2), shared(my_k, count, 1, 3)]
+    second_half = [shared(theirs, count // 2, 0, 4), shared(theirs, count // 2, 1, 5)]
+    onward = [passed(0, 6), passed(1, 7)]
 
     sin, cos = sincos(window[...])
     row = lax.broadcasted_iota(jnp.int32, (2 * N, N), 0)
@@ -210,13 +220,13 @@
     trig[0] = jnp.where(missing == 0, cos, 0.0)
     trig[1] = jnp.where(missing == 0, sin, 0.0)
 
-    def respond_cols(o):
+    def respond_cols(slot, chosen):
         even, odd = [], []
-        edges = [raw[o, part, tall * count :] for part in range(2)]
-        for n in range(count):
+        edges = [raw[slot, part, tall * count :] for part in range(2)]
+        for n in chosen:
             pair = [[], []]
             for part in range(2):
-                turned = raw[o, part, tall * n : tall * (n + 1)]
+                turned = raw[slot, part, tall * n : tall * (n + 1)]
                 extra = cat(
                     [
                         jnp.where(
@@ -235,13 +245,13 @@
             right(cat(odd, 0), fch[:, 2 * N :], fcl[:, 2 * N :]),
         )
 
-    def respond_rows(o, columns, copies):
-        ge, go = columns
+    def respond(o, slot, chosen, copies):
+        ge, go = respond_cols(slot, chosen)
         row = lax.broadcasted_iota(jnp.int32, (N, 2 * N), 0)
         even, odd = [], []
-        for n in range(count):
+        for i in range(len(chosen)):
             pair = [[], []]
-            at = slice(tall * n, tall * (n + 1))
+            at = slice(tall * i, tall * (i + 1))
             for c in (slice(0, N), slice(N, 2 * N)):
                 g = cat([ge[at, c], go[at, c]], 1)
                 extra = jnp.where(row == H, g[N : N + 1], 0.0)
@@ -252,9 +262,10 @@
         for p, x in enumerate((even, odd)):
             half = slice(2 * N * p, 2 * N * (p + 1))
             r = left(frh[half], frl[half], cat(x, 1))
-            for n in range(count):
-                resp[o, n, half] = r[:, 2 * N * n : 2 * N * (n + 1)]
-            copies[p].start()
+            for i, n in enumerate(chosen):
+                resp[o, n, half] = r[:, 2 * N * i : 2 * N * (i + 1)]
+            if copies:
+                copies[p].start()
 
     def members(owners):
         return [(o, n) for o in owners for n in range(count)]
@@ -291,10 +302,7 @@
 
     for load in loads[1 + 2 * count :]:
         load.wait()
-    respond_rows(my_k, respond_cols(0), first_group)
-    to_across.wait_recv()
-    to_around.wait_recv()
-    respond_rows(theirs, respond_cols(1), second_group)
+    respond(my_k, 0, range(count), first_group)
 
     when(has_next, halo[0].wait_recv)
     when(has_prev, halo[1].wait_recv)
@@ -323,9 +331,25 @@
     for copy in first_group:
         copy.wait_recv()
     intensity = fields((my_k, kin))
+
+    @stage
+    def _():
+        to_across.wait_recv()
+        to_around.wait_recv()
+        for copy in onward:
+            copy.start()
+        respond(theirs, 1, range(count), second_half)
+
     intensity = intensity + fields((theirs,))
-    for copy in second_group:
-        copy.wait_recv()
+
+    @stage
+    def _():
+        for copy in onward:
+            copy.wait_recv()
+        respond(theirs_kin, 2, range(count // 2, count), None)
+        for copy in second_half:
+            copy.wait_recv()
+
     intensity = intensity + fields((theirs_kin,))
 
     resist = 1.0 / (1.0 + jnp.exp(-STEEP * (intensity - LEVEL)))
@@ -376,42 +400,44 @@
     e = right(cat([br[:, :N], bi[:, :N]], 1), frh[: 2 * N], frl[: 2 * N])
     o = right(cat([br[:, N:], bi[:, N:]], 1), frh[2 * N :], frl[2 * N :])
     u, v = e + o, e - o
-    gout[0] = u[:, N:] * trig[0] - u[:, :N] * trig[1]
+    gout[...] = u[:, N:] * trig[0] - u[:, :N] * trig[1]
     side = v[:, N:] * trig[2] - v[:, :N] * trig[3]
-    gout[1] = side
     pout[0], pout[1] = pack(side[:H], side[H:N])
+    quarter = H // 2
+    cout[0], cout[1] = pack(side[N : N + quarter], side[N + quarter : N + H])
+    cout[2], cout[3] = pack(side[N + H : N + H + quarter], side[N + H + quarter :])
     low_rows, high_rows = pl.ds(N, H), pl.ds(N + H, H)
     routes = [
-        (gout.at[0, low_rows], (my_s, k_next), up, down),
-        (gout.at[0, high_rows], (my_s, k_prev), down, up),
+        (gout.at[low_rows], (my_s, k_next), up, down),
+        (gout.at[high_rows], (my_s, k_prev), down, up),
         (pout.at[0], (s_next, my_k), has_next, has_prev),
         (pout.at[1], (s_prev, my_k), has_prev, has_next),
-        (gout.at[1, low_rows], (s_next, k_next), has_next & up, has_prev & down),
-        (gout.at[1, low_rows], (s_prev, k_next), has_prev & up, has_next & down),
-        (gout.at[1, high_rows], (s_next, k_prev), has_next & down, has_prev & up),
-        (gout.at[1, high_rows], (s_prev, k_prev), has_prev & down, has_next & up),
+        (cout.at[0], (s_next, k_next), has_next & up, has_prev & down),
+        (cout.at[1], (s_prev, k_next), has_prev & up, has_next & down),
+        (cout.at[2], (s_next, k_prev), has_next & down, has_prev & up),
+        (cout.at[3], (s_prev, k_prev), has_prev & down, has_next & up),
     ]
     rims = [
-        remote(src, rin.at[i], rim_s.at[i], rim_r.at[i], device)
+        remote(src, rin.at[i] if i < 4 else cin.at[i - 4], rim_s.at[i], rim_r.at[i], device)
         for i, (src, device, _, _) in enumerate(routes)
     ]
-    for i in (4, 5, 6, 7, 2, 3, 0, 1):
+    for i in (2, 3, 4, 5, 6, 7, 0, 1):
         when(routes[i][2], rims[i].start)
     for i in range(8):
         when(routes[i][3], rims[i].wait_recv)
     has_low = jnp.where(lane < H, my_s, space - 1 - my_s) > 0
     upper, lower = unpack(rin[2], rin[3])
-    upper = upper + jnp.where(my_k > 0, jnp.where(lane < H, rin[4], rin[5]), 0.0)
-    lower = lower + jnp.where(my_k < groups - 1, jnp.where(lane < H, rin[6], rin[7]), 0.0)
+    upper = upper + jnp.where(down, cat(unpack(cin[0], cin[1]), 0), 0.0)
+    lower = lower + jnp.where(up, cat(unpack(cin[2], cin[3]), 0), 0.0)
     grad_ref[:H] = (
-        gout[0, :H] + jnp.where(my_k > 0, rin[0], 0.0) + jnp.where(has_low, upper, 0.0)
+        gout[:H] + jnp.where(my_k > 0, rin[0], 0.0) + jnp.where(has_low, upper, 0.0)
     )
     grad_ref[H:] = (
-        gout[0, H:N] + jnp.where(my_k < groups - 1, rin[1], 0.0) + jnp.where(has_low, lower, 0.0)
+        gout[H:N] + jnp.where(my_k < groups - 1, rin[1], 0.0) + jnp.where(has_low, lower, 0.0)
     )
     when(has_prev, halo[0].wait_send)
     when(has_next, halo[1].wait_send)
-    for copy in [to_across, to_around] + first_group + second_group:
+    for copy in [to_across, to_around] + first_group + second_half + onward:
         copy.wait_send()
     for i in range(8):
         when(routes[i][2], rims[i].wait_send)
@@ -442,16 +468,18 @@
             pltpu.VMEM((2, N, N), F32),
             pltpu.VMEM((2, N, N), F32),
             pltpu.VMEM((4, 2 * N, N), F32),
-            pltpu.VMEM((2, 2, count * (N + 8) + 8, N), F32),
+            pltpu.VMEM((3, 2, count * (N + 8) + 8, N), F32),
             pltpu.VMEM((groups, count, 4 * N, 2 * N), F32),
             pltpu.VMEM((4 * N, 2 * N), F32),
             pltpu.VMEM((groups, count * N, 2 * N), F32),
             pltpu.VMEM((4 * N, 2 * N), F32),
-            pltpu.VMEM((2, 2 * N, N), F32),
+            pltpu.VMEM((2 * N, N), F32),
             pltpu.VMEM((2, H, N), F32),
-            pltpu.VMEM((8, H, N), F32),
+            pltpu.VMEM((4, H // 2, N), F32),
+            pltpu.VMEM((4, H, N), F32),
+            pltpu.VMEM((4, H // 2, N), F32),
             dma((2,)), dma((2,)),
-            dma((6,)), dma((6,)),
+            dma((8,)), dma((8,)),
             dma((8,)), dma((8,)),
         ],
         compiler_params=pltpu.CompilerParams(

time: 43 us -> 41.9 us (0.974)
  Pallas kernels: 40.1 us -> 39.2 us
    pallas_call x1, Pallas kernels: 40.1 us -> 39.2 us  [body(): pl.pallas_call(functools.partial(kernel, space, groups, far), out_shape=[...]
where the time goes in v3:
time: 41.9 us; the launch traced here: 41.7 us
  Pallas kernels  39.2 us (94%)
  local copies, waits for them, and re-layouts  1.91 us (5%)
  between operations  0.65 us (2%)
    pallas_call x1, Pallas kernels, body(): pl.pallas_call(functools.partial(kernel, space, groups, far), out_shape=[...  39.2 us
    unnamed x4, local copies, waits for them, and re-layouts  1.91 us

profile of v3, /device:TPU:7, one launch (start us, length us, event | category | flops | bytes accessed | tf_op | source)
XLA Modules:
  0.0 41.7 jit_solution(253280526971412320)
XLA Ops:
  0.6 0.0 copy-start
  0.6 0.6 %copy-done = f32[4]{0:T(128)S(1)} copy-done((f32[4]{0:T(128)S(1)}, f32[4]{0:T(128)}, u32[]{:S(2)}) %copy-start) | copy-done | bytes 40
  1.3 39.2 %hopkins.1 = (f32[128,128]{1,0:T(8,128)S(1)}, f32[128,128]{1,0:T(8,128)S(1)}) custom-call(f32[512,128]{1,0:T(8,128)} %phase_hbm.1, s32[512,128]{1,0:T(8,128)} %target_hbm.1, f32[2,129,4,129]{3,2,1,0:T(4,128)} %bitcast.1, f32[4]{0:T(128)S(1)} %copy-done, bf16[256,512]{1,0:T(8,128)(2,1)} %constant.8.clone.fch_hbm, bf16[256,512]{1,0:T(8,128)(2,1)} %constant.9.clone.fcl_hbm, ...), custom_call_target="tpu_custom_call" | custom-call | flops 14000000000 | bytes 4000000 | tf_op jit(solution)/shard_map/hopkins/pallas_call | solution.py:454
  40.5 0.6 %copy.12 = f32[128,128]{1,0:T(8,128)} copy(f32[128,128]{1,0:T(8,128)S(1)} %get-tuple-element.4) | data formatting | bytes 131072
  41.1 0.6 %copy.13 = f32[128,128]{1,0:T(8,128)} copy(f32[128,128]{1,0:T(8,128)S(1)} %get-tuple-element.5) | data formatting | bytes 131072
Async XLA Ops:
  0.6 0.7 %copy-start = (f32[4]{0:T(128)S(1)}, f32[4]{0:T(128)}, u32[]{:S(2)}) copy-start(f32[4]{0:T(128)} %weight_ref.1) | copy-start | bytes 52

commit v4 on v3

--- a/solution.py
+++ b/solution.py
@@ -80,7 +80,7 @@
 def kernel(
     space, groups, far,
     phase_hbm, target_hbm, kern_hbm, weight_ref, fch_hbm, fcl_hbm, frh_hbm, frl_hbm,
-    resist_ref, grad_ref,
+    out_ref,
     phase_ref, target_ref, kern_ref, fch, fcl, frh, frl, load_s,
     window, halo_out, halo_in, trig, raw, resp, spec, field, acc, gout, pout, cout, rin, cin,
     halo_s, halo_r, kern_s, kern_r, rim_s, rim_r,
@@ -98,8 +98,7 @@
     loads = [
         pltpu.make_async_copy(src, dst, load_s.at[i]) for i, (src, dst) in enumerate(pairs)
     ]
-    for load in loads:
-        load.start()
+    loads[0].start()
     tall = N + 8
     my_s = lax.axis_index("space")
     s_next = lax.rem(my_s + 1, space)
@@ -116,10 +115,10 @@
 
     barrier = pltpu.get_barrier_semaphore()
     greeted = [
-        (sibling, None), (across, None), (around, None), (mirror, up & down),
-        ((s_next, my_k), has_next), ((s_prev, my_k), has_prev),
         ((s_next, k_next), has_next & up), ((s_next, k_prev), has_next & down),
         ((s_prev, k_next), has_prev & up), ((s_prev, k_prev), has_prev & down),
+        ((s_next, my_k), has_next), ((s_prev, my_k), has_prev),
+        (around, None), (across, None), (mirror, up & down), (sibling, None),
     ]
 
     def when(condition, action):
@@ -139,6 +138,9 @@
             ),
         )
         expected = expected + (1 if condition is None else jnp.where(condition, 1, 0))
+
+    for load in loads[1:]:
+        load.start()
 
     lane = lax.broadcasted_iota(jnp.int32, (8, N), 1)[:1]
 
@@ -353,7 +355,7 @@
     intensity = intensity + fields((theirs_kin,))
 
     resist = 1.0 / (1.0 + jnp.exp(-STEEP * (intensity - LEVEL)))
-    resist_ref[...] = resist
+    out_ref[0] = resist
     want = target_ref[...].astype(F32)
     factor = 4.0 * STEEP * (resist - want) * resist * (1.0 - resist)
 
@@ -429,10 +431,10 @@
     upper, lower = unpack(rin[2], rin[3])
     upper = upper + jnp.where(down, cat(unpack(cin[0], cin[1]), 0), 0.0)
     lower = lower + jnp.where(up, cat(unpack(cin[2], cin[3]), 0), 0.0)
-    grad_ref[:H] = (
+    out_ref[1, :H] = (
         gout[:H] + jnp.where(my_k > 0, rin[0], 0.0) + jnp.where(has_low, upper, 0.0)
     )
-    grad_ref[H:] = (
+    out_ref[1, H:] = (
         gout[H:N] + jnp.where(my_k < groups - 1, rin[1], 0.0) + jnp.where(has_low, lower, 0.0)
     )
     when(has_prev, halo[0].wait_send)
@@ -451,11 +453,11 @@
     vmem = pl.BlockSpec(memory_space=pltpu.VMEM)
     hbm = pl.BlockSpec(memory_space=pltpu.HBM)
     dma = pltpu.SemaphoreType.DMA
-    return pl.pallas_call(
+    out = pl.pallas_call(
         functools.partial(kernel, space, groups, far),
-        out_shape=[jax.ShapeDtypeStruct((N, cols), F32)] * 2,
+        out_shape=jax.ShapeDtypeStruct((2, N, cols), F32),
         in_specs=[hbm] * 3 + [pl.BlockSpec(memory_space=pltpu.SMEM)] + [hbm] * 4,
-        out_specs=[vmem, vmem],
+        out_specs=vmem,
         scratch_shapes=[
             pltpu.VMEM((rows, N), F32),
             pltpu.VMEM((N, N), jnp.int32),
@@ -490,6 +492,7 @@
         ),
         name="hopkins",
     )(phase, target, jnp.transpose(kernels, (0, 2, 1, 3)), weights, *consts)
+    return (out[0], out[1])
 
 
 def solution(mesh):

time: 41.9 us -> 41.1 us (0.981)
  local copies, waits for them, and re-layouts: 1.91 us -> 1.31 us
    unnamed x4 -> x2, local copies, waits for them, and re-layouts: 1.91 us -> 0.65 us
    squeeze x0 -> x1, local copies, waits for them, and re-layouts: none -> 0.66 us  [body(): return (out[0], out[1])]
where the time goes in v4:
time: 41.1 us; the launch traced here: 41 us
  Pallas kernels  39.1 us (95%)
  local copies, waits for them, and re-layouts  1.31 us (3%)
  between operations  0.65 us (2%)
    pallas_call x1, Pallas kernels, body(): pl.pallas_call(functools.partial(kernel, space, groups, far), out_shape=j...  39.1 us

profile of v4, /device:TPU:7, one launch (start us, length us, event | category | flops | bytes accessed | tf_op | source)
XLA Modules:
  0.0 41.0 jit_solution(15534071510794304160)
XLA Ops:
  0.6 0.0 copy-start
  0.6 0.6 %copy-done = f32[4]{0:T(128)S(1)} copy-done((f32[4]{0:T(128)S(1)}, f32[4]{0:T(128)}, u32[]{:S(2)}) %copy-start) | copy-done | bytes 40
  1.3 39.1 %hopkins.1 = f32[2,128,128]{2,1,0:T(8,128)S(1)} custom-call(f32[512,128]{1,0:T(8,128)} %phase_hbm.1, s32[512,128]{1,0:T(8,128)} %target_hbm.1, f32[2,129,4,129]{3,2,1,0:T(4,128)} %bitcast.5, f32[4]{0:T(128)S(1)} %copy-done, bf16[256,512]{1,0:T(8,128)(2,1)} %constant.8.clone.fch_hbm, bf16[256,512]{1,0:T(8,128)(2,1)} %constant.9.clone.fcl_hbm, ...), custom_call_target="tpu_custom_call" | custom-call | flops 14000000000 | bytes 4000000 | tf_op jit(solution)/shard_map/hopkins/pallas_call | solution.py:456
  40.4 0.7 %slice_bitcast_fusion = (f32[128,128]{1,0:T(8,128)}, f32[128,128]{1,0:T(8,128)}) fusion(f32[2,128,128]{2,1,0:T(8,128)S(1)} %hopkins.1), kind=kLoop, calls=%fused_computation | loop fusion | bytes 262144 | tf_op jit(solution)/shard_map/squeeze | solution.py:495
Async XLA Ops:
  0.6 0.7 %copy-start = (f32[4]{0:T(128)S(1)}, f32[4]{0:T(128)}, u32[]{:S(2)}) copy-start(f32[4]{0:T(128)} %weight_ref.1) | copy-start | bytes 52

commit v5 on v4

--- a/solution.py
+++ b/solution.py
@@ -196,9 +196,16 @@
 
     theirs = flip(my_k, 2)
     to_across = remote(raw.at[0, 0], raw.at[1, 0], kern_s.at[0], kern_r.at[0], across)
-    to_around = remote(raw.at[0, 1], raw.at[1, 1], kern_s.at[1], kern_r.at[1], around)
+    some, most = pl.ds(0, H), pl.ds(H, tall * count + 8 - H)
+    to_around = remote(
+        raw.at[0, 1, most], raw.at[1, 1, most], kern_s.at[1], kern_r.at[1], around
+    )
+    to_share = remote(
+        raw.at[0, 1, some], raw.at[1, 1, some], kern_s.at[8], kern_r.at[8], across
+    )
+    to_around.start()
     to_across.start()
-    to_around.start()
+    to_share.start()
 
     def shared(group, number, parity, index):
         half = resp.at[group, pl.ds(0, number), pl.ds(2 * N * parity, 2 * N)]
@@ -338,6 +345,7 @@
     def _():
         to_across.wait_recv()
         to_around.wait_recv()
+        to_share.wait_recv()
         for copy in onward:
             copy.start()
         respond(theirs, 1, range(count), second_half)
@@ -439,7 +447,7 @@
     )
     when(has_prev, halo[0].wait_send)
     when(has_next, halo[1].wait_send)
-    for copy in [to_across, to_around] + first_group + second_half + onward:
+    for copy in [to_across, to_around, to_share] + first_group + second_half + onward:
         copy.wait_send()
     for i in range(8):
         when(routes[i][2], rims[i].wait_send)
@@ -481,7 +489,7 @@
             pltpu.VMEM((4, H, N), F32),
             pltpu.VMEM((4, H // 2, N), F32),
             dma((2,)), dma((2,)),
-            dma((8,)), dma((8,)),
+            dma((9,)), dma((9,)),
             dma((8,)), dma((8,)),
         ],
         compiler_params=pltpu.CompilerParams(

time: 41.1 us -> 41.2 us (level)
  no operation moved by 1% of the time
where the time goes in v5:
time: 41.2 us; the launch traced here: 41 us
  Pallas kernels  39.1 us (95%)
  local copies, waits for them, and re-layouts  1.31 us (3%)
  between operations  0.65 us (2%)
    pallas_call x1, Pallas kernels, body(): pl.pallas_call(functools.partial(kernel, space, groups, far), out_shape=j...  39.1 us

profile of v5, /device:TPU:7, one launch (start us, length us, event | category | flops | bytes accessed | tf_op | source)
XLA Modules:
  0.0 41.0 jit_solution(3795922760483842333)
XLA Ops:
  0.6 0.0 copy-start
  0.6 0.6 %copy-done = f32[4]{0:T(128)S(1)} copy-done((f32[4]{0:T(128)S(1)}, f32[4]{0:T(128)}, u32[]{:S(2)}) %copy-start) | copy-done | bytes 40
  1.3 39.1 %hopkins.1 = f32[2,128,128]{2,1,0:T(8,128)S(1)} custom-call(f32[512,128]{1,0:T(8,128)} %phase_hbm.1, s32[512,128]{1,0:T(8,128)} %target_hbm.1, f32[2,129,4,129]{3,2,1,0:T(4,128)} %bitcast.5, f32[4]{0:T(128)S(1)} %copy-done, bf16[256,512]{1,0:T(8,128)(2,1)} %constant.8.clone.fch_hbm, bf16[256,512]{1,0:T(8,128)(2,1)} %constant.9.clone.fcl_hbm, ...), custom_call_target="tpu_custom_call" | custom-call | flops 14000000000 | bytes 4000000 | tf_op jit(solution)/shard_map/hopkins/pallas_call | solution.py:464
  40.4 0.7 %slice_bitcast_fusion = (f32[128,128]{1,0:T(8,128)}, f32[128,128]{1,0:T(8,128)}) fusion(f32[2,128,128]{2,1,0:T(8,128)S(1)} %hopkins.1), kind=kLoop, calls=%fused_computation | loop fusion | bytes 262144 | tf_op jit(solution)/shard_map/squeeze | solution.py:503
Async XLA Ops:
  0.6 0.7 %copy-start = (f32[4]{0:T(128)S(1)}, f32[4]{0:T(128)}, u32[]{:S(2)}) copy-start(f32[4]{0:T(128)} %weight_ref.1) | copy-start | bytes 52
